TPU v7x, 128 devices: a whole 4x4x4 slice. The times are simulated.
128 devices in a mesh: row: 8 (over x, core), col: 16 (over z, y).
Axes of the slice: x: 4, y: 4, z: 4, core: 2. Of those that a mesh axis runs over, the one named last changes fastest.
Arguments:
- density: bfloat16 [6144, 6144], P('row', 'col'), may hold values from -5 to 5
- strips: bfloat16 [16384, 8, 128], P(('row', 'col')), may hold values from -5 to 5
- dest_device: int32 [16384, 1], P(('row', 'col')), may hold values from 0 to 127; in each aligned block of 128 rows (0 to 127, 128 to 255, ...) at most 2 rows name the same one
- atom_slot: int32 [16384], P(('row', 'col')), may hold values from 0 to 95
- block_slot: int32 [16384], P(('row', 'col')), may hold values from 0 to 2
- patterns: int32 [3, 48, 48], replicated, may hold values 0 or 1
Outputs:
- density_next: float32 [6144, 6144], P('row', 'col')
- response_next: float32 [6144, 6144], P('row', 'col')
Inputs may be any that keep to these rules, and one draw needn't show every extreme that they name: `dest_device`: of the 128 strips of one device, at most 2 name the same owner, and some owner is named that often.
All inputs are finite; a program needn't handle non-finite values.
Results may differ from a plain program's by a relative error of at most 0.0036.
Values may be sent and summed in bfloat16 or wider, within the bound.
A program may use at most 128 MiB of HBM per device.

v0:
```python
import math
import jax
import jax.numpy as jnp
from jax import lax
from jax.sharding import PartitionSpec as P

STEPS = 2
CAPACITY = 2


def tile_kept(patterns, which, row_offset, col_offset, block_rows, block_cols, block_width):
    window = lax.dynamic_slice(patterns[which], (row_offset, col_offset), (block_rows, block_cols))
    global_rows = row_offset + lax.iota(jnp.int32, block_rows)
    global_cols = col_offset + lax.iota(jnp.int32, block_cols)
    diagonal = (global_rows[:, None] == global_cols[None, :]).astype(jnp.int32)
    kept = jnp.maximum(window, diagonal).astype(jnp.float32)
    return jnp.repeat(jnp.repeat(kept, block_width, axis=0), block_width, axis=1)


def products(zeroth, linear):
    col_zero, col_first = (
        lax.all_gather(zeroth, "row", axis=0, tiled=True),
        lax.all_gather(linear, "row", axis=0, tiled=True),
    )
    pieces = (
        lax.all_gather(zeroth, "col", axis=1, tiled=True),
        lax.all_gather(linear, "col", axis=1, tiled=True),
    )
    square = jnp.dot(pieces[0], col_zero, preferred_element_type=jnp.float32)
    left_part = jnp.dot(pieces[0], col_first, preferred_element_type=jnp.float32)
    right_part = jnp.dot(pieces[1], col_zero, preferred_element_type=jnp.float32)
    return (square, left_part + right_part)


def on_device(density, strips, dest_device, atom_slot, block_slot, patterns):
    tile_rows, tile_cols = density.shape
    mesh_rows = lax.axis_size("row")
    mesh_cols = lax.axis_size("col")
    devices = mesh_rows * mesh_cols
    matrix_order = tile_rows * mesh_rows
    atom_width = strips.shape[1]
    block_width = strips.shape[2]
    block_rows = tile_rows // block_width
    block_cols = tile_cols // block_width
    row_offset = lax.axis_index("row") * block_rows
    col_offset = lax.axis_index("col") * block_cols
    kept_zero = tile_kept(patterns, 0, row_offset, col_offset, block_rows, block_cols, block_width)
    kept_first = tile_kept(patterns, 1, row_offset, col_offset, block_rows, block_cols, block_width)
    kept_field = tile_kept(patterns, 2, row_offset, col_offset, block_rows, block_cols, block_width)
    capacity = CAPACITY
    targets = dest_device[:, 0]
    matches = (targets[:, None] == lax.iota(jnp.int32, devices)[None, :]).astype(jnp.int32)
    before = jnp.cumsum(matches, axis=0) - matches
    ranking = jnp.sum(before * matches, axis=1)
    position = targets * capacity + ranking
    sent_strips = (
        jnp.zeros((devices * capacity, atom_width, block_width), strips.dtype)
        .at[position]
        .set(strips)
    )
    sent_atoms = jnp.full((devices * capacity,), -1, jnp.int32).at[position].set(atom_slot)
    sent_blocks = jnp.zeros((devices * capacity,), jnp.int32).at[position].set(block_slot)
    arrived = (
        lax.all_to_all(
            sent_strips.reshape(devices, capacity, atom_width, block_width),
            ("row", "col"),
            split_axis=0,
            concat_axis=0,
            tiled=True,
        ),
        lax.all_to_all(
            sent_atoms.reshape(devices, capacity),
            ("row", "col"),
            split_axis=0,
            concat_axis=0,
            tiled=True,
        ),
        lax.all_to_all(
            sent_blocks.reshape(devices, capacity),
            ("row", "col"),
            split_axis=0,
            concat_axis=0,
            tiled=True,
        ),
    )
    recv_strips = arrived[0].reshape(-1, atom_width * block_width)
    recv_atoms = arrived[1].reshape(-1)
    recv_blocks = arrived[2].reshape(-1)
    atoms_here = tile_rows // atom_width
    atom_match = recv_atoms[:, None] == lax.iota(jnp.int32, atoms_here)[None, :]
    block_match = recv_blocks[:, None] == lax.iota(jnp.int32, block_cols)[None, :]
    placing = (
        (atom_match[:, :, None] & block_match[:, None, :])
        .astype(jnp.bfloat16)
        .reshape(-1, atoms_here * block_cols)
    )
    summed = lax.dot_general(
        placing, recv_strips, (((0,), (0,)), ((), ())), preferred_element_type=jnp.float32
    )
    h_field = (
        summed.reshape(atoms_here, block_cols, atom_width, block_width)
        .transpose(0, 2, 1, 3)
        .reshape(tile_rows, tile_cols)
    )
    linear = (-(kept_field * h_field)).astype(jnp.bfloat16)
    zeroth = density
    inv_root = 1.0 / math.sqrt(matrix_order)
    new_zeroth = None
    new_linear = None
    for iteration in range(STEPS):
        square, crossed = products(zeroth, linear)
        if iteration % 2 == 0:
            new_zeroth = kept_zero * (square * inv_root)
            new_linear = kept_first * (crossed * inv_root)
        else:
            new_zeroth = kept_zero * (2.0 * zeroth.astype(jnp.float32) - square * inv_root)
            new_linear = kept_first * (2.0 * linear.astype(jnp.float32) - crossed * inv_root)
        zeroth = new_zeroth.astype(jnp.bfloat16)
        linear = new_linear.astype(jnp.bfloat16)
    return (new_zeroth, new_linear)


def solution(mesh):
    return jax.shard_map(
        on_device,
        mesh=mesh,
        in_specs=(
            P("row", "col"),
            P(("row", "col"), None, None),
            P(("row", "col"), None),
            P(("row", "col")),
            P(("row", "col")),
            P(),
        ),
        out_specs=(P("row", "col"), P("row", "col")),
        check_vma=False,
    )
```

profile of v0, /device:TPU:0, one launch (start us, length us, event | category | flops | bytes accessed | tf_op | source)
XLA Modules:
  0.0 541.6 jit_solution(12071236785653305353)
XLA Ops:
  7.2 0.7 all-gather.11.cloned.1.call-update
  7.9 0.7 fusion.14
  8.7 0.2 reduce_window_sum.11
  8.8 0.8 select_reduce_fusion
  9.7 0.7 fusion.18
  10.3 1.1 scatter_custom_fusion.1
  11.4 0.8 all_to_all.17
  12.2 11.1 %all-to-all-start.1 = ((s32[128,1,2]{2,1,0:T(1,128)}), s32[128,1,2]{2,1,0:T(1,128)S(1)}, u32[]{:S(2)}, u32[]{:S(2)}) async-start(s32[128,1,2]{2,1,0:T(1,128)} %bitcast.10), calls=%async_computation.1 | async-start | bytes 131072 | tf_op jit(solution)/shard_map/all_to_all | solution.py:78
  23.4 0.8 fusion.23
  24.1 0.1 constant_dynamic-slice_fusion
  24.2 0.1 copy.30
  24.3 0.1 copy.31
  24.4 0.1 constant_dynamic-slice_fusion.2
  24.5 0.1 copy.27
  24.6 0.1 fusion.17
  24.7 1.1 scatter_custom_fusion
  25.8 0.8 all_to_all.15
  26.6 6.2 %all-to-all-done.1 = s32[128,1,2]{2,1,0:T(1,128)S(1)} async-done(((s32[128,1,2]{2,1,0:T(1,128)}), s32[128,1,2]{2,1,0:T(1,128)S(1)}, u32[]{:S(2)}, u32[]{:S(2)}) %all-to-all-start.1) | async-done | bytes 1056 | tf_op jit(solution)/shard_map/all_to_all | solution.py:78
  32.8 4.6 all-to-all-start
  37.4 0.1 broadcast_bitcast_fusion
  37.5 0.9 broadcast_in_dim.49
  38.3 13.3 %scatter_fusion = bf16[256,8,128]{2,1,0:T(8,128)(2,1)} fusion(bf16[256,8,128]{2,1,0:T(8,128)(2,1)} %broadcast_in_dim.49, s32[128]{0:T(128)S(1)} %fusion.18, bf16[128,8,128]{2,1,0:T(8,128)(2,1)S(1)} %copy-done.2), kind=kCustom, calls=%fused_computation.2 | custom fusion | bytes 786944 | tf_op jit(solution)/shard_map/scatter | solution.py:59
  51.6 0.6 broadcast.69
  52.2 0.8 reduce.6
  53.1 0.1 eq.91
  53.2 9.8 %all-to-all-start.2 = ((bf16[128,2,8,128]{3,2,1,0:T(8,128)(2,1)}), bf16[128,2,8,128]{3,2,1,0:T(8,128)(2,1)S(1)}, u32[]{:S(2)}, u32[]{:S(2)}) async-start(bf16[128,2,8,128]{3,2,1,0:T(8,128)(2,1)} %bitcast.13), calls=%async_computation.2 | async-start | bytes 1048576 | tf_op jit(solution)/shard_map/all_to_all | solution.py:64
  63.0 0.0 all-gather.19.cloned.1.call-start
  63.1 0.8 reduce.7
  63.9 0.1 eq.87
  64.1 0.1 broadcast_and_fusion
  64.2 0.1 and.22
  64.4 0.1 dot_general.34
  64.5 12.2 %all-to-all-done.2 = bf16[128,2,8,128]{3,2,1,0:T(8,128)(2,1)S(1)} async-done(((bf16[128,2,8,128]{3,2,1,0:T(8,128)(2,1)}), bf16[128,2,8,128]{3,2,1,0:T(8,128)(2,1)S(1)}, u32[]{:S(2)}, u32[]{:S(2)}) %all-to-all-start.2) | async-done | bytes 524320 | tf_op jit(solution)/shard_map/all_to_all | solution.py:64
  76.6 0.1 copy.57
  76.7 0.2 copy.34
  76.9 0.4 convolution_bitcast_fusion.1
  77.3 0.7 copy.56
  78.0 0.4 copy.37
  78.4 0.9 fusion.12
  79.3 0.7 all-gather.17.cloned.1.call-update
  80.1 0.5 all-gather.9.cloned.1.call-update
  80.7 0.1 broadcast_bitcast_fusion.1
  80.7 0.1 broadcast_in_dim.21
  80.8 0.4 copy.40
  81.2 69.7 %all-gather.19.cloned.1.call-done = bf16[768,6144]{0,1:T(8,128)(2,1)} async-done(((bf16[768,384]{0,1:T(8,128)(2,1)}), bf16[768,6144]{0,1:T(8,128)(2,1)}) %all-gather.19.cloned.1.call-update) | async-done | bytes 9437200 | tf_op jit(solution)/shard_map/all_gather | solution.py:27
  150.9 9.0 %fusion.24 = f32[768,384]{1,0:T(8,128)S(1)} fusion(bf16[768,6144]{0,1:T(8,128)(2,1)} %all-gather.19.cloned.1.call-done, bf16[6144,384]{1,0:T(8,128)(2,1)} %all-gather.11.cloned.1.call-done), kind=kOutput, calls=%fused_computation.56 | convolution fusion | flops 3623878656 | bytes 15335424 | tf_op jit(solution)/shard_map/dot_general | solution.py:31
  159.9 27.1 %all-gather.17.cloned.1.call-done = bf16[6144,384]{0,1:T(8,128)(2,1)} async-done(((bf16[768,384]{0,1:T(8,128)(2,1)}), bf16[6144,384]{0,1:T(8,128)(2,1)}) %all-gather.17.cloned.1.call-update) | async-done | bytes 4718608 | tf_op jit(solution)/shard_map/all_gather | solution.py:23
  187.1 85.9 %all-gather.9.cloned.1.call-done = bf16[768,6144]{1,0:T(8,128)(2,1)} async-done(((bf16[768,384]{1,0:T(8,128)(2,1)}), bf16[768,6144]{1,0:T(8,128)(2,1)}) %all-gather.9.cloned.1.call-update) | async-done | bytes 9437200 | tf_op jit(solution)/shard_map/all_gather | solution.py:26
  272.9 9.8 %fusion.9 = bf16[768,384]{1,0:T(8,128)(2,1)} fusion(f32[768,384]{1,0:T(8,128)S(1)} %copy.40, f32[768,384]{1,0:T(8,128)S(1)} %fusion.24, bf16[6144,384]{0,1:T(8,128)(2,1)} %all-gather.17.cloned.1.call-done, bf16[768,6144]{1,0:T(8,128)(2,1)} %all-gather.9.cloned.1.call-done), kind=kOutput, calls=%fused_computation.17 | convolution fusion | flops 3625058304 | bytes 17104896 | tf_op jit(solution)/shard_map/dot_general | solution.py:30
  282.8 0.2 all-gather.13.cloned.1.call-start
  283.0 0.1 broadcast_bitcast_fusion.2
  283.1 0.1 broadcast_in_dim.19
  283.2 0.4 copy.29
  283.5 9.7 %fusion.10 = bf16[768,384]{1,0:T(8,128)(2,1)} fusion(f32[768,384]{1,0:T(8,128)S(1)} %copy.29, bf16[768,6144]{1,0:T(8,128)(2,1)} %all-gather.9.cloned.1.call-done, bf16[6144,384]{1,0:T(8,128)(2,1)} %all-gather.11.cloned.1.call-done), kind=kOutput, calls=%fused_computation.18 | convolution fusion | flops 3624763392 | bytes 15925248 | tf_op jit(solution)/shard_map/dot_general | solution.py:29
  293.3 0.0 all-gather.15.cloned.1.call-start
  293.3 0.7 all-gather.15.cloned.1.call-update
  294.1 0.7 all-gather.23.cloned.1.call-update
  294.8 21.6 %all-gather.21.cloned.1.call-done = bf16[6144,384]{1,0:T(8,128)(2,1)} async-done(((bf16[768,384]{1,0:T(8,128)(2,1)}), bf16[6144,384]{1,0:T(8,128)(2,1)}) %all-gather.21.cloned.1.call-update) | async-done | bytes 4718608 | tf_op jit(solution)/shard_map/all_gather | solution.py:23
  316.4 86.4 %all-gather.13.cloned.1.call-done = bf16[768,6144]{1,0:T(8,128)(2,1)} async-done(((bf16[768,384]{1,0:T(8,128)(2,1)}), bf16[768,6144]{1,0:T(8,128)(2,1)}) %all-gather.13.cloned.1.call-update) | async-done | bytes 9437200 | tf_op jit(solution)/shard_map/all_gather | solution.py:26
  402.9 9.8 %fusion.25 = f32[768,384]{1,0:T(8,128)} fusion(bf16[768,6144]{1,0:T(8,128)(2,1)} %all-gather.13.cloned.1.call-done, bf16[6144,384]{1,0:T(8,128)(2,1)} %all-gather.21.cloned.1.call-done), kind=kOutput, calls=%fused_computation.57 | convolution fusion | flops 3623878656 | bytes 15335424 | tf_op jit(solution)/shard_map/dot_general | solution.py:30
  412.6 26.0 %all-gather.15.cloned.1.call-done = bf16[6144,384]{1,0:T(8,128)(2,1)} async-done(((bf16[768,384]{1,0:T(8,128)(2,1)}), bf16[6144,384]{1,0:T(8,128)(2,1)}) %all-gather.15.cloned.1.call-update) | async-done | bytes 4718608 | tf_op jit(solution)/shard_map/all_gather | solution.py:22
  438.7 9.8 %fusion.2 = f32[768,384]{1,0:T(8,128)} fusion(f32[768,384]{1,0:T(8,128)S(1)} %copy.29, bf16[768,6144]{1,0:T(8,128)(2,1)} %all-gather.13.cloned.1.call-done, bf16[6144,384]{1,0:T(8,128)(2,1)} %all-gather.15.cloned.1.call-done, bf16[768,384]{1,0:T(8,128)(2,1)S(1)} %copy-done.1), kind=kOutput, calls=%fused_computation.9 | convolution fusion | flops 3625353216 | bytes 17104896 | tf_op jit(solution)/shard_map/dot_general | solution.py:29
  448.5 76.2 %all-gather.23.cloned.1.call-done = bf16[768,6144]{1,0:T(8,128)(2,1)} async-done(((bf16[768,384]{1,0:T(8,128)(2,1)}), bf16[768,6144]{1,0:T(8,128)(2,1)}) %all-gather.23.cloned.1.call-update) | async-done | bytes 9437200 | tf_op jit(solution)/shard_map/all_gather | solution.py:27
  524.7 10.1 %fusion.8 = f32[768,384]{1,0:T(8,128)} fusion(f32[768,384]{1,0:T(8,128)S(1)} %copy.40, f32[768,384]{1,0:T(8,128)} %fusion.25, bf16[768,6144]{1,0:T(8,128)(2,1)} %all-gather.23.cloned.1.call-done, bf16[6144,384]{1,0:T(8,128)(2,1)} %all-gather.15.cloned.1.call-done, bf16[768,384]{1,0:T(8,128)(2,1)S(1)} %copy-done), kind=kOutput, calls=%fused_computation.16 | convolution fusion | flops 3625648128 | bytes 18284544 | tf_op jit(solution)/shard_map/dot_general | solution.py:31
  (23 shorter events, 0.3 us)
Async XLA Ops:
  7.2 31.2 %copy-start.2 = (bf16[128,8,128]{2,1,0:T(8,128)(2,1)S(1)}, bf16[128,8,128]{2,1,0:T(8,128)(2,1)}, u32[]{:S(2)}) copy-start(bf16[128,8,128]{2,1,0:T(8,128)(2,1)} %param.7) | copy-start | bytes 786436
  7.2 74.1 %all-gather.11.cloned.1.call-start = ((), (), s32[]{:S(2)}) async-start(), calls=%async_computation.4 | async-start | bytes 5308416 | tf_op jit(solution)/shard_map/all_gather | solution.py:22
  12.2 20.6 %all-to-all-start.1 = ((s32[128,1,2]{2,1,0:T(1,128)}), s32[128,1,2]{2,1,0:T(1,128)S(1)}, u32[]{:S(2)}, u32[]{:S(2)}) async-start(s32[128,1,2]{2,1,0:T(1,128)} %bitcast.10), calls=%async_computation.1 | async-start | bytes 131072 | tf_op jit(solution)/shard_map/all_to_all | solution.py:78
  32.8 20.5 %all-to-all-start = ((s32[128,1,2]{2,1,0:T(1,128)}), s32[128,1,2]{2,1,0:T(1,128)S(1)}, u32[]{:S(2)}, u32[]{:S(2)}) async-start(s32[128,1,2]{2,1,0:T(1,128)} %bitcast.9), calls=%async_computation | async-start | bytes 131072 | tf_op jit(solution)/shard_map/all_to_all | solution.py:71
  53.2 23.4 %all-to-all-start.2 = ((bf16[128,2,8,128]{3,2,1,0:T(8,128)(2,1)}), bf16[128,2,8,128]{3,2,1,0:T(8,128)(2,1)S(1)}, u32[]{:S(2)}, u32[]{:S(2)}) async-start(bf16[128,2,8,128]{3,2,1,0:T(8,128)(2,1)} %bitcast.13), calls=%async_computation.2 | async-start | bytes 1048576 | tf_op jit(solution)/shard_map/all_to_all | solution.py:64
  63.0 87.9 %all-gather.19.cloned.1.call-start = ((), (), s32[]{:S(2)}) async-start(), calls=%async_computation.8 | async-start | bytes 10027008 | tf_op jit(solution)/shard_map/all_gather | solution.py:27
  79.3 107.8 %all-gather.17.cloned.1.call-start = ((), (), s32[]{:S(2)}) async-start(), calls=%async_computation.7 | async-start | bytes 5308416 | tf_op jit(solution)/shard_map/all_gather | solution.py:23
  80.0 192.9 %all-gather.9.cloned.1.call-start = ((), (), s32[]{:S(2)}) async-start(), calls=%async_computation.3 | async-start | bytes 10027008 | tf_op jit(solution)/shard_map/all_gather | solution.py:26
  80.6 235.8 %all-gather.21.cloned.1.call-start = ((), (), s32[]{:S(2)}) async-start(), calls=%async_computation.9 | async-start | bytes 5308416 | tf_op jit(solution)/shard_map/all_gather | solution.py:23
  282.8 120.1 %all-gather.13.cloned.1.call-start = ((), (), s32[]{:S(2)}) async-start(), calls=%async_computation.5 | async-start | bytes 10027008 | tf_op jit(solution)/shard_map/all_gather | solution.py:26
  293.3 145.4 %all-gather.15.cloned.1.call-start = ((), (), s32[]{:S(2)}) async-start(), calls=%async_computation.6 | async-start | bytes 5308416 | tf_op jit(solution)/shard_map/all_gather | solution.py:22
  294.0 230.6 %all-gather.23.cloned.1.call-start = ((), (), s32[]{:S(2)}) async-start(), calls=%async_computation.10 | async-start | bytes 10027008 | tf_op jit(solution)/shard_map/all_gather | solution.py:27
  294.8 143.9 %copy-start.1 = (bf16[768,384]{1,0:T(8,128)(2,1)S(1)}, bf16[768,384]{1,0:T(8,128)(2,1)}, u32[]{:S(2)}) copy-start(bf16[768,384]{1,0:T(8,128)(2,1)} %fusion.10) | copy-start | bytes 1769476
  412.6 112.0 %copy-start = (bf16[768,384]{1,0:T(8,128)(2,1)S(1)}, bf16[768,384]{1,0:T(8,128)(2,1)}, u32[]{:S(2)}) copy-start(bf16[768,384]{1,0:T(8,128)(2,1)} %fusion.9) | copy-start | bytes 1769476
Sparse Core Ops, SparseCore 0:
  9.7 38.0 all-gather.10
  79.4 71.4 all-gather.18
  153.2 33.8 all-gather.16
  189.0 83.8 all-gather.8
  282.9 33.4 all-gather.20
  319.0 83.8 all-gather.12
  405.1 33.4 all-gather.14
  440.8 83.8 all-gather.22
where the time goes:
time: 542 us
  waiting for transfers between devices  415 us (77%)
  matrix products  58.5 us (11%)
  starting transfers between devices  26 us (5%)
  local copies, waits for them, and re-layouts  22.7 us (4%)
  between operations  14.4 us (3%)
    all_gather x2, waiting for transfers between devices, products(): lax.all_gather(zeroth, 'col', axis=1, tiled=True)  172 us
    all_gather x2, waiting for transfers between devices, products(): lax.all_gather(linear, 'col', axis=1, tiled=True)  146 us
    all_gather x2, waiting for transfers between devices, products(): lax.all_gather(linear, 'row', axis=0, tiled=True)  48.8 us
    all_gather x2, waiting for transfers between devices, products(): lax.all_gather(zeroth, 'row', axis=0, tiled=True)  26 us
    dot_general x2, matrix products, products(): jnp.dot(pieces[0], col_first, preferred_element_type=jnp.float32)  19.6 us
    dot_general x2, matrix products, products(): square = jnp.dot(pieces[0], col_zero, preferred_element_type=jnp.float32)  19.5 us
    dot_general x2, matrix products, products(): jnp.dot(pieces[1], col_zero, preferred_element_type=jnp.float32)  19.1 us
    scatter x1, local copies, waits for them, and re-layouts, on_device(): sent_strips = jnp.zeros((devices * capacity, atom_width, block_width), st...  13.3 us
  transfers between devices with their start and end apart: 11, of which 9 were waited for; matrix products, arithmetic and copies ran while one was open for 12% of the time, Pallas kernels for 0%

commit v1 on v0

--- a/solution.py
+++ b/solution.py
@@ -6,6 +6,11 @@
 
 STEPS = 2
 CAPACITY = 2
+
+
+def gather_by_exchange(x, axis, dim):
+    copies = jnp.concatenate([x] * lax.axis_size(axis), axis=dim)
+    return lax.all_to_all(copies, axis, dim, dim, tiled=True)
 
 
 def tile_kept(patterns, which, row_offset, col_offset, block_rows, block_cols, block_width):
@@ -19,7 +24,7 @@
 
 def products(zeroth, linear):
     col_zero, col_first = (
-        lax.all_gather(zeroth, "row", axis=0, tiled=True),
+        gather_by_exchange(zeroth, "row", 0),
         lax.all_gather(linear, "row", axis=0, tiled=True),
     )
     pieces = (

time: 542 us -> 425 us (0.78)
  waiting for transfers between devices: 415 us -> 214 us
  blocking collectives: 0 us -> 59.3 us
  local copies, waits for them, and re-layouts: 22.7 us -> 43.9 us
    all_gather x2, waiting for transfers between devices: 172 us -> 0.01 us  [products(): lax.all_gather(zeroth, 'col', axis=1, tiled=True)]
    all_gather x2, waiting for transfers between devices: 146 us -> 85 us  [products(): lax.all_gather(linear, 'col', axis=1, tiled=True)]
    all_to_all x0 -> x1, blocking collectives: none -> 59.3 us  [gather_by_exchange(): return lax.all_to_all(copies, axis, dim, dim, tiled=True)]
    all_to_all x0 -> x1, waiting for transfers between devices: none -> 55 us  [gather_by_exchange(): return lax.all_to_all(copies, axis, dim, dim, tiled=True)]
    all_gather x2 -> x0, waiting for transfers between devices: 26 us -> none  [products(): lax.all_gather(zeroth, 'row', axis=0, tiled=True)]
    unnamed x13 -> x30, local copies, waits for them, and re-layouts: 0.34 us -> 11.4 us
    all_to_all x0 -> x2, local copies, waits for them, and re-layouts: none -> 9.29 us  [gather_by_exchange(): return lax.all_to_all(copies, axis, dim, dim, tiled=True)]
  transfers between devices with their start and end apart: 11 -> 10, of which waited for: 9 -> 7; matrix products, arithmetic and copies ran while one was open for 12% -> 21% of each run, Pallas kernels for 0% -> 0%
where the time goes in v1:
time: 425 us; the launch traced here: 423 us
  waiting for transfers between devices  214 us (50%)
  blocking collectives  59.3 us (14%)
  matrix products  55.1 us (13%)
  local copies, waits for them, and re-layouts  43.9 us (10%)
  starting transfers between devices  30.5 us (7%)
  between operations  14.4 us (3%)
  other arithmetic  5.14 us (1%)
    all_gather x2, waiting for transfers between devices, products(): lax.all_gather(linear, 'col', axis=1, tiled=True)  85 us
    all_to_all x1, blocking collectives, gather_by_exchange(): return lax.all_to_all(copies, axis, dim, dim, tiled=True)  59.3 us
    all_to_all x1, waiting for transfers between devices, gather_by_exchange(): return lax.all_to_all(copies, axis, dim, dim, tiled=True)  55 us
    all_gather x2, waiting for transfers between devices, products(): lax.all_gather(linear, 'row', axis=0, tiled=True)  54.1 us
    dot_general x2, matrix products, products(): square = jnp.dot(pieces[0], col_zero, preferred_element_type=jnp.float32)  19 us
    dot_general x2, matrix products, products(): jnp.dot(pieces[0], col_first, preferred_element_type=jnp.float32)  18.3 us
    dot_general x2, matrix products, products(): jnp.dot(pieces[1], col_zero, preferred_element_type=jnp.float32)  17.5 us
    scatter x1, local copies, waits for them, and re-layouts, on_device(): sent_strips = jnp.zeros((devices * capacity, atom_width, block_width), st...  14 us
  transfers between devices with their start and end apart: 10, of which 7 were waited for; matrix products, arithmetic and copies ran while one was open for 21% of the time, Pallas kernels for 0%

profile of v1, /device:TPU:0, one launch (start us, length us, event | category | flops | bytes accessed | tf_op | source)
XLA Modules:
  0.0 422.8 jit_solution(11591837071736019821)
XLA Ops:
  7.2 0.7 all-gather.7.cloned.1.call-update
  7.9 0.7 fusion.11
  8.6 0.2 reduce_window_sum.11
  8.8 0.8 select_reduce_fusion
  9.6 0.7 fusion.15
  10.3 1.1 scatter_custom_fusion.1
  11.4 0.8 all_to_all.39
  12.2 11.1 %all-to-all-start.3 = ((s32[128,1,2]{2,1,0:T(1,128)}), s32[128,1,2]{2,1,0:T(1,128)S(1)}, u32[]{:S(2)}, u32[]{:S(2)}) async-start(s32[128,1,2]{2,1,0:T(1,128)} %bitcast.14), calls=%async_computation.3 | async-start | bytes 131072 | tf_op jit(solution)/shard_map/all_to_all | solution.py:83
  23.4 0.8 fusion.20
  24.2 0.1 copy.51
  24.5 0.1 copy.47
  24.7 1.1 scatter_custom_fusion
  25.8 0.8 all_to_all.37
  26.5 6.2 %all-to-all-done.3 = s32[128,1,2]{2,1,0:T(1,128)S(1)} async-done(((s32[128,1,2]{2,1,0:T(1,128)}), s32[128,1,2]{2,1,0:T(1,128)S(1)}, u32[]{:S(2)}, u32[]{:S(2)}) %all-to-all-start.3) | async-done | bytes 1056 | tf_op jit(solution)/shard_map/all_to_all | solution.py:83
  32.8 4.6 %all-to-all-start.2 = ((s32[128,1,2]{2,1,0:T(1,128)}), s32[128,1,2]{2,1,0:T(1,128)S(1)}, u32[]{:S(2)}, u32[]{:S(2)}) async-start(s32[128,1,2]{2,1,0:T(1,128)} %bitcast.13), calls=%async_computation.2 | async-start | bytes 131072 | tf_op jit(solution)/shard_map/all_to_all | solution.py:76
  37.4 0.9 broadcast_in_dim.49
  38.3 14.0 %scatter_fusion = bf16[256,8,128]{2,1,0:T(8,128)(2,1)} fusion(bf16[256,8,128]{2,1,0:T(8,128)(2,1)} %broadcast_in_dim.49, s32[128]{0:T(128)S(1)} %fusion.15, bf16[128,8,128]{2,1,0:T(8,128)(2,1)} %param.7), kind=kCustom, calls=%fused_computation.2 | custom fusion | bytes 786944 | tf_op jit(solution)/shard_map/scatter | solution.py:64
  52.3 0.5 broadcast.74
  52.8 0.8 reduce.6
  53.6 0.1 eq.91
  53.8 9.7 %all-to-all-start.4 = ((bf16[128,2,8,128]{3,2,1,0:T(8,128)(2,1)}), bf16[128,2,8,128]{3,2,1,0:T(8,128)(2,1)S(1)}, u32[]{:S(2)}, u32[]{:S(2)}) async-start(bf16[128,2,8,128]{3,2,1,0:T(8,128)(2,1)} %bitcast.17), calls=%async_computation.4 | async-start | bytes 1048576 | tf_op jit(solution)/shard_map/all_to_all | solution.py:69
  63.6 0.8 reduce.7
  64.4 0.1 eq.87
  64.5 0.1 broadcast_and_fusion
  64.7 0.1 and.22
  64.9 12.2 %all-to-all-done.4 = bf16[128,2,8,128]{3,2,1,0:T(8,128)(2,1)S(1)} async-done(((bf16[128,2,8,128]{3,2,1,0:T(8,128)(2,1)}), bf16[128,2,8,128]{3,2,1,0:T(8,128)(2,1)S(1)}, u32[]{:S(2)}, u32[]{:S(2)}) %all-to-all-start.4) | async-done | bytes 524320 | tf_op jit(solution)/shard_map/all_to_all | solution.py:69
  77.2 0.2 copy.55
  77.5 0.4 convolution_bitcast_fusion.1
  77.8 0.7 copy.85
  78.5 0.4 copy.58
  78.9 0.9 fusion.9
  79.9 0.7 all-gather.11.cloned.1.call-update
  80.6 0.1 constant_dynamic-update-slice_fusion.6
  80.7 0.1 constant_dynamic-update-slice_fusion.5
  80.8 0.1 constant_dynamic-update-slice_fusion.4
  80.9 0.1 constant_dynamic-update-slice_fusion.3
  81.0 0.1 constant_dynamic-update-slice_fusion.2
  81.4 2.2 copy-done.3
  83.6 4.6 %all-to-all-start = ((bf16[8,768,384]{2,1,0:T(8,128)(2,1)}), bf16[8,768,384]{2,1,0:T(8,128)(2,1)}, u32[]{:S(2)}, u32[]{:S(2)}) async-start(bf16[8,768,384]{2,1,0:T(8,128)(2,1)} %bitcast.113), calls=%async_computation | async-start | bytes 9437184 | tf_op jit(solution)/shard_map/all_to_all | solution.py:13
  88.2 0.2 all-gather.9.cloned.1.call-start
  88.5 55.0 %all-to-all-done = bf16[8,768,384]{2,1,0:T(8,128)(2,1)} async-done(((bf16[8,768,384]{2,1,0:T(8,128)(2,1)}), bf16[8,768,384]{2,1,0:T(8,128)(2,1)}, u32[]{:S(2)}, u32[]{:S(2)}) %all-to-all-start) | async-done | bytes 4718624 | tf_op jit(solution)/shard_map/all_to_all | solution.py:13
  143.5 10.3 %constant_dynamic-update-slice_fusion.15 = (bf16[6144,384]{0,1:T(8,128)(2,1)}, bf16[768,384]{0,1:T(8,128)(2,1)}) fusion(bf16[6144,384]{1,0:T(8,128)(2,1)} %bitcast.3, bf16[768,6144]{1,0:T(8,128)(2,1)} %all-gather.7.cloned.1.call-done, f32[768,3]{0,1:T(4,128)S(1)} %bitcast.120), kind=kOutput, calls=%fused_computation.47 | convolution fusion | flops 3624763392 | bytes 15344640 | tf_op jit(solution)/shard_map/dot_general | solution.py:34
  153.9 25.1 %all-gather.13.cloned.1.call-done = bf16[768,6144]{0,1:T(8,128)(2,1)} async-done(((bf16[768,384]{0,1:T(8,128)(2,1)}), bf16[768,6144]{0,1:T(8,128)(2,1)}) %all-gather.13.cloned.1.call-update) | async-done | bytes 9437200 | tf_op jit(solution)/shard_map/all_gather | solution.py:32
  179.0 8.7 %fusion.21 = f32[768,384]{0,1:T(8,128)S(1)} fusion(bf16[768,6144]{0,1:T(8,128)(2,1)} %all-gather.13.cloned.1.call-done, bf16[6144,384]{1,0:T(8,128)(2,1)} %bitcast.3), kind=kOutput, calls=%fused_computation.74 | convolution fusion | flops 3623878656 | bytes 15335424 | tf_op jit(solution)/shard_map/dot_general | solution.py:36
  187.7 27.4 %all-gather.11.cloned.1.call-done = bf16[6144,384]{0,1:T(8,128)(2,1)} async-done(((bf16[768,384]{0,1:T(8,128)(2,1)}), bf16[6144,384]{0,1:T(8,128)(2,1)}) %all-gather.11.cloned.1.call-update) | async-done | bytes 4718608 | tf_op jit(solution)/shard_map/all_gather | solution.py:28
  215.1 9.8 %fusion.6 = bf16[768,384]{0,1:T(8,128)(2,1)} fusion(f32[768,384]{0,1:T(8,128)S(1)} %fusion.21, bf16[6144,384]{0,1:T(8,128)(2,1)} %all-gather.11.cloned.1.call-done, bf16[768,6144]{1,0:T(8,128)(2,1)} %all-gather.7.cloned.1.call-done, f32[768,3]{0,1:T(4,128)S(1)} %bitcast.122), kind=kOutput, calls=%fused_computation.19 | convolution fusion | flops 3625058304 | bytes 15934464 | tf_op jit(solution)/shard_map/dot_general | solution.py:35
  225.0 0.5 all-gather.15.cloned.1.call-update
  225.6 0.9 constant_dynamic-update-slice_fusion.14
  226.5 0.9 constant_dynamic-update-slice_fusion.13
  227.4 1.0 constant_dynamic-update-slice_fusion.12
  228.3 0.9 constant_dynamic-update-slice_fusion.11
  229.2 0.9 constant_dynamic-update-slice_fusion.10
  230.2 0.9 constant_dynamic-update-slice_fusion.9
  231.1 1.0 constant_dynamic-update-slice_fusion.8
  232.1 2.6 copy.84
  234.7 59.3 %all_to_all.47 = bf16[8,768,384]{1,2,0:T(8,128)(2,1)} all-to-all(bf16[8,768,384]{1,2,0:T(8,128)(2,1)S(1)} %bitcast.109), channel_id=1, replica_groups=mesh['row'=8,'col'=16] {'row'}, dimensions={0} | all-to-all | bytes 9437184 | tf_op jit(solution)/shard_map/all_to_all | solution.py:13
  294.0 6.6 %copy.49 = bf16[8,768,384]{2,1,0:T(8,128)(2,1)} copy(bf16[8,768,384]{1,2,0:T(8,128)(2,1)} %all_to_all.47) | data formatting | bytes 9437184 | tf_op jit(solution)/shard_map/all_to_all | solution.py:13
  300.7 8.8 %bitcast_multiply_fusion.2 = f32[768,384]{0,1:T(8,128)S(1)} fusion(bf16[768,6144]{0,1:T(8,128)(2,1)} %all-gather.9.cloned.1.call-done, bf16[6144,384]{1,0:T(8,128)(2,1)} %bitcast.110, bf16[768,384]{0,1:T(8,128)(2,1)S(1)} %copy-done, f32[768,3]{0,1:T(4,128)S(1)} %bitcast.121), kind=kOutput, calls=%fused_computation.6 | convolution fusion | flops 3625353216 | bytes 15934464 | tf_op jit(solution)/shard_map/dot_general | solution.py:34
  309.4 1.4 copy.62
  310.8 59.9 %all-gather.17.cloned.1.call-done = bf16[768,6144]{0,1:T(8,128)(2,1)} async-done(((bf16[768,384]{0,1:T(8,128)(2,1)}), bf16[768,6144]{0,1:T(8,128)(2,1)}) %all-gather.17.cloned.1.call-update) | async-done | bytes 9437200 | tf_op jit(solution)/shard_map/all_gather | solution.py:32
  370.7 8.8 %fusion.22 = f32[768,384]{0,1:T(8,128)S(1)} fusion(bf16[768,6144]{0,1:T(8,128)(2,1)} %all-gather.17.cloned.1.call-done, bf16[6144,384]{1,0:T(8,128)(2,1)} %bitcast.111), kind=kOutput, calls=%fused_computation.75 | convolution fusion | flops 3623878656 | bytes 15335424 | tf_op jit(solution)/shard_map/dot_general | solution.py:36
  379.5 26.7 %all-gather.15.cloned.1.call-done = bf16[6144,384]{0,1:T(8,128)(2,1)} async-done(((bf16[768,384]{0,1:T(8,128)(2,1)}), bf16[6144,384]{0,1:T(8,128)(2,1)}) %all-gather.15.cloned.1.call-update) | async-done | bytes 4718608 | tf_op jit(solution)/shard_map/all_gather | solution.py:28
  406.2 8.4 %bitcast_multiply_fusion = f32[768,384]{0,1:T(8,128)S(1)} fusion(f32[768,384]{0,1:T(8,128)S(1)} %fusion.22, bf16[6144,384]{0,1:T(8,128)(2,1)} %all-gather.15.cloned.1.call-done, bf16[768,6144]{0,1:T(8,128)(2,1)} %all-gather.9.cloned.1.call-done, bf16[768,384]{0,1:T(8,128)(2,1)S(1)} %copy-done.2, f32[768,3]{0,1:T(4,128)S(1)} %bitcast.123), kind=kOutput, calls=%fused_computation.4 | convolution fusion | flops 3625648128 | bytes 17114112 | tf_op jit(solution)/shard_map/dot_general | solution.py:35
  414.6 1.4 copy.63
  (37 shorter events, 1.3 us)
Async XLA Ops:
  7.2 136.3 %all-gather.7.cloned.1.call-start = ((), (), s32[]{:S(2)}) async-start(), calls=%async_computation.5 | async-start | bytes 10027008 | tf_op jit(solution)/shard_map/all_gather | solution.py:31
  12.2 20.6 %all-to-all-start.3 = ((s32[128,1,2]{2,1,0:T(1,128)}), s32[128,1,2]{2,1,0:T(1,128)S(1)}, u32[]{:S(2)}, u32[]{:S(2)}) async-start(s32[128,1,2]{2,1,0:T(1,128)} %bitcast.14), calls=%async_computation.3 | async-start | bytes 131072 | tf_op jit(solution)/shard_map/all_to_all | solution.py:83
  32.8 21.0 %all-to-all-start.2 = ((s32[128,1,2]{2,1,0:T(1,128)}), s32[128,1,2]{2,1,0:T(1,128)S(1)}, u32[]{:S(2)}, u32[]{:S(2)}) async-start(s32[128,1,2]{2,1,0:T(1,128)} %bitcast.13), calls=%async_computation.2 | async-start | bytes 131072 | tf_op jit(solution)/shard_map/all_to_all | solution.py:76
  53.8 23.4 %all-to-all-start.4 = ((bf16[128,2,8,128]{3,2,1,0:T(8,128)(2,1)}), bf16[128,2,8,128]{3,2,1,0:T(8,128)(2,1)S(1)}, u32[]{:S(2)}, u32[]{:S(2)}) async-start(bf16[128,2,8,128]{3,2,1,0:T(8,128)(2,1)} %bitcast.17), calls=%async_computation.4 | async-start | bytes 1048576 | tf_op jit(solution)/shard_map/all_to_all | solution.py:69
  63.5 115.5 %all-gather.13.cloned.1.call-start = ((), (), s32[]{:S(2)}) async-start(), calls=%async_computation.8 | async-start | bytes 10027008 | tf_op jit(solution)/shard_map/all_gather | solution.py:32
  77.4 3.1 copy-start.1
  79.8 135.3 %all-gather.11.cloned.1.call-start = ((), (), s32[]{:S(2)}) async-start(), calls=%async_computation.7 | async-start | bytes 5308416 | tf_op jit(solution)/shard_map/all_gather | solution.py:28
  81.4 2.2 copy-start.3
  83.6 59.9 %all-to-all-start = ((bf16[8,768,384]{2,1,0:T(8,128)(2,1)}), bf16[8,768,384]{2,1,0:T(8,128)(2,1)}, u32[]{:S(2)}, u32[]{:S(2)}) async-start(bf16[8,768,384]{2,1,0:T(8,128)(2,1)} %bitcast.113), calls=%async_computation | async-start | bytes 9437184 | tf_op jit(solution)/shard_map/all_to_all | solution.py:13
  88.2 212.5 %all-gather.9.cloned.1.call-start = ((), (), s32[]{:S(2)}) async-start(), calls=%async_computation.6 | async-start | bytes 10027008 | tf_op jit(solution)/shard_map/all_gather | solution.py:31
  153.8 217.0 %all-gather.17.cloned.1.call-start = ((), (), s32[]{:S(2)}) async-start(), calls=%async_computation.10 | async-start | bytes 10027008 | tf_op jit(solution)/shard_map/all_gather | solution.py:32
  215.1 10.4 %copy-start = (bf16[768,384]{0,1:T(8,128)(2,1)S(1)}, bf16[768,384]{0,1:T(8,128)(2,1)}, u32[]{:S(2)}) copy-start(bf16[768,384]{0,1:T(8,128)(2,1)} %get-tuple-element.17) | copy-start | bytes 1769476
  225.0 181.2 %all-gather.15.cloned.1.call-start = ((), (), s32[]{:S(2)}) async-start(), calls=%async_computation.9 | async-start | bytes 5308416 | tf_op jit(solution)/shard_map/all_gather | solution.py:28
  310.8 95.3 %copy-start.2 = (bf16[768,384]{0,1:T(8,128)(2,1)S(1)}, bf16[768,384]{0,1:T(8,128)(2,1)}, u32[]{:S(2)}) copy-start(bf16[768,384]{0,1:T(8,128)(2,1)} %fusion.6) | copy-start | bytes 1769476
Sparse Core Ops, SparseCore 0:
  10.1 92.5 all-gather.6
  105.4 73.5 all-gather.12
  181.3 33.8 all-gather.10
  217.7 75.6 all-gather.8
  295.4 75.2 all-gather.16
  372.3 33.8 all-gather.14
